TPU v7x, 32 devices: a whole 2x2x4 slice. The times are simulated.
32 devices in a mesh: dp: 4 (over x, core), sp: 8 (over z, y).
Axes of the slice: x: 2, y: 2, z: 4, core: 2. Of those that a mesh axis runs over, the one named last changes fastest.
Arguments:
- tokens: bfloat16 [4, 2048, 768], P('dp', 'sp'), may hold values from -24 to 24
- cotangent: bfloat16 [4, 2048, 768], P('dp', 'sp'), may hold values from -6 to 6
- routes: int32 [4, 2048, 1], P('dp', 'sp'), may hold values from 0 to 3; in each aligned block of 256 rows (0 to 255, 256 to 511, ..., all dimensions but the last counted through in order) at most 128 rows name the same one
- buckets: int32 [4095], replicated, may hold values from 0 to 31, as said below
- gain_attn: bfloat16 [768], P('sp'), may hold values from 0.099609375 to 1.8984375
- w_qkv: bfloat16 [768, 2304], P('sp'), may hold values from -0.109375 to 0.109375
- w_out: bfloat16 [768, 768], P('sp'), may hold values from -2.5 to 2.5
- bias_table: bfloat16 [32, 12], replicated, may hold values from -4 to 4
- gain_ffn: bfloat16 [768], P('sp'), may hold values from 0.099609375 to 1.8984375
- router: bfloat16 [768, 4], P('sp'), may hold values from -0.15625 to 0.15625
- expert_in: bfloat16 [4, 768, 3072], P(None, 'sp'), may hold values from -0.21875 to 0.21875
- expert_out: bfloat16 [4, 3072, 768], P(None, 'sp'), may hold values from -0.75 to 0.75
Outputs:
- mixed: bfloat16 [4, 2048, 768], P('dp', 'sp')
- tokens_grad: float32 [4, 2048, 768], P('dp', 'sp')
- gain_attn_grad: float32 [768], P('sp')
- w_qkv_grad: float32 [768, 2304], P('sp')
- w_out_grad: float32 [768, 768], P('sp')
- bias_table_grad: float32 [32, 12], replicated
- gain_ffn_grad: float32 [768], P('sp')
- router_grad: float32 [768, 4], P('sp')
- expert_in_grad: float32 [4, 768, 3072], P(None, 'sp')
- expert_out_grad: float32 [4, 3072, 768], P(None, 'sp')
Inputs may be any that keep to these rules, and one draw needn't show every extreme that they name: `routes`: each token names one expert; among the tokens of one device's piece of a sequence (aligned blocks of 2048 / 8 positions) no expert is named more than 128 times. `buckets`: entry r + 2047 is the bucket of the relative position r, key position minus query position.
All inputs are finite; a program needn't handle non-finite values.
Results may differ from a plain program's by a relative error of at most 0.02.
Values may be sent and summed in bfloat16 or wider, within the bound.
A program may use at most 256 MiB of HBM per device.

v0:
```python
import jax
import jax.numpy as jnp
from jax import lax
from jax.sharding import PartitionSpec as P

HIGHEST_PRECISION = lax.Precision.HIGHEST
epsilon = 1e-06


def rms_scale(values):
    return lax.rsqrt(jnp.mean(values * values, axis=-1, keepdims=True) + epsilon)


def norm_back(values, scale, gain, grad_out):
    weighted = gain * grad_out
    grad_in = scale * weighted - values * scale**3 * jnp.mean(
        weighted * values, axis=-1, keepdims=True
    )
    grad_gain = jnp.sum(grad_out * values * scale, axis=(0, 1))
    return (grad_in, grad_gain)


def bucket_onehot(buckets, count, query_start, query_count, key_count):
    length = (buckets.shape[0] + 1) // 2
    key_positions = jnp.arange(key_count, dtype=jnp.int32)
    query_positions = query_start + jnp.arange(query_count, dtype=jnp.int32)
    offsets = key_positions[None, :] - query_positions[:, None] + (length - 1)
    pair_buckets = jnp.take(buckets, offsets, axis=0)
    return (pair_buckets[:, :, None] == jnp.arange(count, dtype=jnp.int32)[None, None, :]).astype(
        jnp.bfloat16
    )


def split_heads(values, heads):
    return values.reshape(values.shape[0], values.shape[1], heads, values.shape[2] // heads)


def body(
    tokens,
    cotangent,
    routes,
    buckets,
    gain_attn,
    w_qkv,
    w_out,
    bias_table,
    gain_ffn,
    router,
    expert_in,
    expert_out,
):
    heads = bias_table.shape[1]
    bucket_count = bias_table.shape[0]
    seq_count, piece, width = tokens.shape
    attn_set = (
        lax.all_gather(gain_attn, "sp", axis=0, tiled=True),
        lax.all_gather(w_qkv, "sp", axis=0, tiled=True),
        lax.all_gather(w_out, "sp", axis=0, tiled=True),
    )
    ffn_set = (
        lax.all_gather(gain_ffn, "sp", axis=0, tiled=True),
        lax.all_gather(router, "sp", axis=0, tiled=True),
        lax.all_gather(expert_in, "sp", axis=1, tiled=True),
        lax.all_gather(expert_out, "sp", axis=1, tiled=True),
    )
    inputs = tokens.astype(jnp.float32)
    scale_one = rms_scale(inputs)
    normed_one = (inputs * scale_one * attn_set[0].astype(jnp.float32)).astype(jnp.bfloat16)
    projected = jnp.einsum(
        "spd,de->spe", normed_one, attn_set[1], preferred_element_type=jnp.float32
    ).astype(jnp.bfloat16)
    queries = projected[:, :, :width]
    keys = projected[:, :, width : 2 * width]
    values = projected[:, :, 2 * width :]
    keys_all, values_all = (
        lax.all_gather(keys, "sp", axis=1, tiled=True),
        lax.all_gather(values, "sp", axis=1, tiled=True),
    )
    length = keys_all.shape[1]
    start = lax.axis_index("sp") * piece
    near_onehot = bucket_onehot(buckets, bucket_count, start, piece, length)
    bias_rows = jnp.einsum(
        "ijc,ch->hij", near_onehot, bias_table, preferred_element_type=jnp.float32
    )
    query_heads = split_heads(queries, heads)
    scores = (
        jnp.einsum(
            "sihd,sjhd->shij",
            query_heads,
            split_heads(keys_all, heads),
            preferred_element_type=jnp.float32,
        )
        + bias_rows[None]
    )
    top_score = jnp.max(scores, axis=-1, keepdims=True)
    log_total = top_score + jnp.log(jnp.sum(jnp.exp(scores - top_score), axis=-1, keepdims=True))
    probs_low = jnp.exp(scores - log_total).astype(jnp.bfloat16)
    attended = jnp.einsum(
        "shij,sjhd->sihd",
        probs_low,
        split_heads(values_all, heads),
        preferred_element_type=jnp.float32,
    )
    attended = attended.reshape(seq_count, piece, width).astype(jnp.bfloat16)
    middle = inputs + jnp.einsum(
        "spd,de->spe", attended, attn_set[2], preferred_element_type=jnp.float32
    )
    gain_two = ffn_set[0].astype(jnp.float32)
    scale_two = rms_scale(middle)
    normed_two = (middle * scale_two * gain_two).astype(jnp.bfloat16)
    experts = ffn_set[1].shape[1]
    logits = jnp.einsum("spd,de->spe", normed_two, ffn_set[1], preferred_element_type=jnp.float32)
    gates_all = jax.nn.softmax(logits, axis=-1)
    chosen_int = (routes == jnp.arange(experts, dtype=jnp.int32)[None, None, :]).astype(jnp.int32)
    chosen = chosen_int.astype(jnp.float32)
    gate = jnp.sum(gates_all * chosen, axis=-1, keepdims=True)
    capacity = 2 * piece // experts
    place = jnp.sum((jnp.cumsum(chosen_int, axis=1) - 1) * chosen_int, axis=-1)
    slots = (place[:, :, None] == jnp.arange(capacity, dtype=jnp.int32)[None, None, :]).astype(
        jnp.float32
    )
    dispatch = chosen[:, :, :, None] * slots[:, :, None, :]
    dispatch_low = dispatch.astype(jnp.bfloat16)
    buffers = jnp.einsum(
        "stec,std->secd", dispatch_low, normed_two, preferred_element_type=jnp.float32
    ).astype(jnp.bfloat16)
    hidden_in = jnp.einsum(
        "secd,edf->secf", buffers, ffn_set[2], preferred_element_type=jnp.float32
    )
    activated = jax.nn.gelu(hidden_in).astype(jnp.bfloat16)
    expert_outs = jnp.einsum(
        "secf,efd->secd", activated, ffn_set[3], preferred_element_type=jnp.float32
    )
    returned = jnp.einsum("stec,secd->std", dispatch, expert_outs, precision=HIGHEST_PRECISION)
    mixed = (middle + gate * returned).astype(jnp.bfloat16)
    grad_out = cotangent.astype(jnp.float32)
    grad_gate = jnp.sum(grad_out * returned, axis=-1, keepdims=True)
    grad_returned = (gate * grad_out).astype(jnp.bfloat16)
    grad_outs = jnp.einsum(
        "stec,std->secd", dispatch_low, grad_returned, preferred_element_type=jnp.float32
    ).astype(jnp.bfloat16)
    ffn_back = (
        lax.all_gather(gain_ffn, "sp", axis=0, tiled=True),
        lax.all_gather(router, "sp", axis=0, tiled=True),
        lax.all_gather(expert_in, "sp", axis=1, tiled=True),
        lax.all_gather(expert_out, "sp", axis=1, tiled=True),
    )
    grad_w_down = jnp.einsum(
        "secf,secd->efd", activated, grad_outs, preferred_element_type=jnp.float32
    )
    grad_act = jnp.einsum(
        "secd,efd->secf", grad_outs, ffn_back[3], preferred_element_type=jnp.float32
    )
    grad_hidden = jax.vjp(jax.nn.gelu, hidden_in)[1](grad_act)[0].astype(jnp.bfloat16)
    grad_w_up = jnp.einsum(
        "secd,secf->edf", buffers, grad_hidden, preferred_element_type=jnp.float32
    )
    grad_buffers = jnp.einsum(
        "secf,edf->secd", grad_hidden, ffn_back[2], preferred_element_type=jnp.float32
    )
    grad_normed_two = jnp.einsum(
        "stec,secd->std", dispatch, grad_buffers, precision=HIGHEST_PRECISION
    )
    grad_logits = grad_gate * gate * (chosen - gates_all)
    grad_router = jnp.einsum(
        "spd,spe->de", normed_two.astype(jnp.float32), grad_logits, precision=HIGHEST_PRECISION
    )
    grad_normed_two = grad_normed_two + jnp.einsum(
        "spe,de->spd", grad_logits, ffn_back[1].astype(jnp.float32), precision=HIGHEST_PRECISION
    )
    grad_middle, grad_gain_two = norm_back(
        middle, scale_two, ffn_back[0].astype(jnp.float32), grad_normed_two
    )
    grad_middle = grad_out + grad_middle
    ffn_shares = (
        lax.psum_scatter(
            grad_gain_two.astype(jnp.bfloat16), "sp", scatter_dimension=0, tiled=True
        ).astype(jnp.float32),
        lax.psum_scatter(
            grad_router.astype(jnp.bfloat16), "sp", scatter_dimension=0, tiled=True
        ).astype(jnp.float32),
        lax.psum_scatter(
            grad_w_up.astype(jnp.bfloat16), "sp", scatter_dimension=1, tiled=True
        ).astype(jnp.float32),
        lax.psum_scatter(
            grad_w_down.astype(jnp.bfloat16), "sp", scatter_dimension=1, tiled=True
        ).astype(jnp.float32),
    )
    ffn_grads = (
        lax.psum(ffn_shares[0].astype(jnp.bfloat16), "dp").astype(jnp.float32),
        lax.psum(ffn_shares[1].astype(jnp.bfloat16), "dp").astype(jnp.float32),
        lax.psum(ffn_shares[2].astype(jnp.bfloat16), "dp").astype(jnp.float32),
        lax.psum(ffn_shares[3].astype(jnp.bfloat16), "dp").astype(jnp.float32),
    )
    attn_back = (
        lax.all_gather(gain_attn, "sp", axis=0, tiled=True),
        lax.all_gather(w_qkv, "sp", axis=0, tiled=True),
        lax.all_gather(w_out, "sp", axis=0, tiled=True),
    )
    keys_back, values_back = (
        lax.all_gather(keys, "sp", axis=1, tiled=True),
        lax.all_gather(values, "sp", axis=1, tiled=True),
    )
    grad_branch = grad_middle.astype(jnp.bfloat16)
    grad_w_out = jnp.einsum(
        "spd,spe->de", attended, grad_branch, preferred_element_type=jnp.float32
    )
    grad_attended = jnp.einsum(
        "spe,de->spd", grad_branch, attn_back[2], preferred_element_type=jnp.float32
    ).astype(jnp.bfloat16)
    grad_heads = split_heads(grad_attended, heads)
    key_heads = split_heads(keys_back, heads)
    value_heads = split_heads(values_back, heads)
    scores_back = (
        jnp.einsum("sihd,sjhd->shij", query_heads, key_heads, preferred_element_type=jnp.float32)
        + bias_rows[None]
    )
    probs_back = jnp.exp(scores_back - log_total)
    grad_probs = jnp.einsum(
        "sihd,sjhd->shij", grad_heads, value_heads, preferred_element_type=jnp.float32
    )
    row_dot = jnp.sum(probs_back * grad_probs, axis=-1, keepdims=True)
    grad_scores = (probs_back * (grad_probs - row_dot)).astype(jnp.bfloat16)
    grad_queries = jnp.einsum(
        "shij,sjhd->sihd", grad_scores, key_heads, preferred_element_type=jnp.float32
    )
    grad_queries = grad_queries.reshape(seq_count, piece, width).astype(jnp.bfloat16)
    grad_table = jnp.einsum(
        "shij,ijc->ch", grad_scores, near_onehot, preferred_element_type=jnp.float32
    )
    grad_keys_part = jnp.einsum(
        "shij,sihd->sjhd", grad_scores, query_heads, preferred_element_type=jnp.float32
    )
    grad_values_part = jnp.einsum(
        "shij,sihd->sjhd",
        probs_back.astype(jnp.bfloat16),
        grad_heads,
        preferred_element_type=jnp.float32,
    )
    grad_keys, grad_values = (
        lax.psum_scatter(
            grad_keys_part.reshape(seq_count, length, width).astype(jnp.bfloat16),
            "sp",
            scatter_dimension=1,
            tiled=True,
        ).astype(jnp.float32),
        lax.psum_scatter(
            grad_values_part.reshape(seq_count, length, width).astype(jnp.bfloat16),
            "sp",
            scatter_dimension=1,
            tiled=True,
        ).astype(jnp.float32),
    )
    grad_projected = jnp.concatenate(
        (grad_queries, grad_keys.astype(jnp.bfloat16), grad_values.astype(jnp.bfloat16)), axis=-1
    )
    grad_w_qkv = jnp.einsum(
        "spd,spe->de", normed_one, grad_projected, preferred_element_type=jnp.float32
    )
    grad_normed_one = jnp.einsum(
        "spe,de->spd", grad_projected, attn_back[1], preferred_element_type=jnp.float32
    )
    grad_inputs, grad_gain_one = norm_back(
        inputs, scale_one, attn_back[0].astype(jnp.float32), grad_normed_one
    )
    grad_inputs = grad_middle + grad_inputs
    attn_shares = (
        lax.psum_scatter(
            grad_gain_one.astype(jnp.bfloat16), "sp", scatter_dimension=0, tiled=True
        ).astype(jnp.float32),
        lax.psum_scatter(
            grad_w_qkv.astype(jnp.bfloat16), "sp", scatter_dimension=0, tiled=True
        ).astype(jnp.float32),
        lax.psum_scatter(
            grad_w_out.astype(jnp.bfloat16), "sp", scatter_dimension=0, tiled=True
        ).astype(jnp.float32),
    )
    attn_grads = (
        lax.psum(attn_shares[0].astype(jnp.bfloat16), "dp").astype(jnp.float32),
        lax.psum(attn_shares[1].astype(jnp.bfloat16), "dp").astype(jnp.float32),
        lax.psum(attn_shares[2].astype(jnp.bfloat16), "dp").astype(jnp.float32),
    )
    table_total = lax.psum(grad_table, ("dp", "sp"))
    return (
        mixed,
        grad_inputs,
        attn_grads[0],
        attn_grads[1],
        attn_grads[2],
        table_total,
        ffn_grads[0],
        ffn_grads[1],
        ffn_grads[2],
        ffn_grads[3],
    )


def solution(mesh):
    return jax.shard_map(
        body,
        mesh=mesh,
        in_specs=(
            P("dp", "sp", None),
            P("dp", "sp", None),
            P("dp", "sp", None),
            P(),
            P("sp"),
            P("sp", None),
            P("sp", None),
            P(),
            P("sp"),
            P("sp", None),
            P(None, "sp", None),
            P(None, "sp", None),
        ),
        out_specs=(
            P("dp", "sp", None),
            P("dp", "sp", None),
            P("sp"),
            P("sp", None),
            P("sp", None),
            P(),
            P("sp"),
            P("sp", None),
            P(None, "sp", None),
            P(None, "sp", None),
        ),
        check_vma=False,
    )
```

profile of v0, /device:TPU:0, one launch (start us, length us, event | category | flops | bytes accessed | tf_op | source)
XLA Modules:
  0.0 6510.9 jit_solution(1802090756316261149)
XLA Ops:
  11.7 23.8 all-reduce.5
  37.2 41.1 all-gather.8.cloned.1.call-done
  89.4 5122.7 %gather_fusion = s32[524288]{0:T(1024)} fusion(s32[4095]{0:T(1024)S(1)} %copy-done, s32[524288]{0:T(1024)S(1)} %broadcast_clamp_fusion), kind=kCustom, calls=%fused_computation | custom fusion | bytes 6291456 | tf_op jit(solution)/shard_map/jit(_take)/gather | solution.py:28
  5214.8 18.3 all-gather
  5235.9 15.1 fusion.1
  5259.2 28.6 fusion.104
  5320.6 11.9 fusion.106
  5332.5 13.1 fusion.12
  5345.6 11.7 fusion.22
  5377.0 13.9 convolution_convert_fusion.4
  5391.0 17.2 multiply_reduce_fusion
  5408.2 17.5 multiply_convert_fusion
  5443.5 20.0 reduce-scatter.12.cloned.1.call-done
  5463.5 77.9 %reduce-scatter.10.cloned.1.call-done = bf16[1,256,768]{1,2,0:T(8,128)(2,1)} async-done(((bf16[1,2048,768]{1,2,0:T(8,128)(2,1)}), bf16[1,256,768]{1,2,0:T(8,128)(2,1)}) %reduce-scatter.10.cloned.1.call-update) | async-done | bytes 393232 | tf_op jit(solution)/shard_map/reduce_scatter | solution.py:241
  5545.9 10.7 convolution_convert_fusion.1
  5557.7 12.3 convolution_convert_fusion
  5572.6 35.5 reduce-scatter.16.cloned.1.call-done
  5608.2 81.9 %reduce-scatter.14.cloned.1.call-done = bf16[96,2304]{1,0:T(8,128)(2,1)} async-done(((bf16[768,2304]{1,0:T(8,128)(2,1)}), bf16[96,2304]{1,0:T(8,128)(2,1)}) %reduce-scatter.14.cloned.1.call-update) | async-done | bytes 442384 | tf_op jit(solution)/shard_map/reduce_scatter | solution.py:271
  5690.1 316.8 %reduce-scatter.18.cloned.1.call-done = bf16[4,96,3072]{2,1,0:T(8,128)(2,1)} async-done(((bf16[4,768,3072]{2,1,0:T(8,128)(2,1)}), bf16[4,96,3072]{2,1,0:T(8,128)(2,1)}) %reduce-scatter.18.cloned.1.call-update) | async-done | bytes 2359312 | tf_op jit(solution)/shard_map/reduce_scatter | solution.py:182
  6006.9 316.3 %reduce-scatter.20.cloned.1.call-done = bf16[4,384,768]{2,1,0:T(8,128)(2,1)} async-done(((bf16[4,3072,768]{2,1,0:T(8,128)(2,1)}), bf16[4,384,768]{2,1,0:T(8,128)(2,1)}) %reduce-scatter.20.cloned.1.call-update) | async-done | bytes 2359312 | tf_op jit(solution)/shard_map/reduce_scatter | solution.py:185
  6323.2 27.0 fusion.35
  6350.3 39.8 psum.59
  6394.3 21.5 all-reduce.4
  6425.3 67.8 %all-reduce.10.cloned.1.call-done = (bf16[96,2304]{1,0:T(8,128)(2,1)}, bf16[96,768]{1,0:T(8,128)(2,1)}, bf16[4,96,3072]{2,1,0:T(8,128)(2,1)}, bf16[4,384,768]{2,1,0:T(8,128)(2,1)}) async-done(((bf16[96,2304]{1,0:T(8,128)(2,1)}, bf16[96,768]{1,0:T(8,128)(2,1)}, bf16[4,96,3072]{2,1,0:T(8,128)(2,1)}, bf16[4,384,768]{2,1,0:T(8,128)(2,1)}), (bf16[96,2304]{1,0:T(8,128)(2,1)}, bf16[96,768]{1,0:T(8,128)(2,1)}, ...) | async-done | bytes 5308432 | tf_op jit(solution)/shard_map/psum | solution.py:280
  (232 shorter events, 132.0 us)
Async XLA Ops:
  7.2 71.1 %all-gather.8.cloned.1.call-start = ((), (), s32[]{:S(2)}) async-start(), calls=%async_computation.7 | async-start | bytes 3981312 | tf_op jit(solution)/shard_map/all_gather | solution.py:57
  7.9 5243.3 %all-gather.10.cloned.1.call-start = ((), (), s32[]{:S(2)}) async-start(), calls=%async_computation.8 | async-start | bytes 3538944 | tf_op jit(solution)/shard_map/all_gather | solution.py:77
  82.6 5171.9 %all-gather.12.cloned.1.call-start = ((), (), s32[]{:S(2)}) async-start(), calls=%async_computation.9 | async-start | bytes 3538944 | tf_op jit(solution)/shard_map/all_gather | solution.py:76
  83.4 5225.7 %all-gather.14.cloned.1.call-start = ((), (), s32[]{:S(2)}) async-start(), calls=%async_computation.10 | async-start | bytes 1327104 | tf_op jit(solution)/shard_map/all_gather | solution.py:58
  83.9 5236.6 %all-gather.16.cloned.1.call-start = ((), (), s32[]{:S(2)}) async-start(), calls=%async_computation.11 | async-start | bytes 21233664 | tf_op jit(solution)/shard_map/all_gather | solution.py:63
  84.5 5247.9 %all-gather.18.cloned.1.call-start = ((), (), s32[]{:S(2)}) async-start(), calls=%async_computation.12 | async-start | bytes 21233664 | tf_op jit(solution)/shard_map/all_gather | solution.py:64
  85.1 5378.4 %reduce-scatter.12.cloned.1.call-start = ((), (), s32[]{:S(2)}) async-start(), calls=%async_computation.14 | async-start | bytes 3538944 | tf_op jit(solution)/shard_map/reduce_scatter | solution.py:247
  89.4 5124.5 %copy-start.58 = (bf16[768]{0:T(1024)(128)(2,1)S(1)}, bf16[768]{0:T(1024)(128)(2,1)}, u32[]{:S(2)}) copy-start(bf16[768]{0:T(1024)(128)(2,1)} %get-tuple-element.17) | copy-start | bytes 4612
  89.4 5125.1 %copy-start.41 = (s32[1,4,2,1]{3,2,1,0:T(2,128)S(1)}, s32[1,4,2,1]{3,2,1,0:T(2,128)}, u32[]{:S(2)}) copy-start(s32[1,4,2,1]{3,2,1,0:T(2,128)} %slice.25) | copy-start | bytes 100
  89.4 5125.4 %copy-start.59 = (bf16[96,4]{0,1:T(4,128)(2,1)S(1)}, bf16[96,4]{0,1:T(4,128)(2,1)}, u32[]{:S(2)}) copy-start(bf16[96,4]{0,1:T(4,128)(2,1)} %param.21) | copy-start | bytes 2308
  89.4 5144.4 %copy-start.30 = (s32[1,256,1]{1,2,0:T(1,128)S(1)}, s32[1,256,1]{1,2,0:T(1,128)}, u32[]{:S(2)}) copy-start(s32[1,256,1]{1,2,0:T(1,128)} %param.14) | copy-start | bytes 3076
  89.4 5144.4 %copy-start.42 = (s32[1,4,256]{2,1,0:T(4,128)S(1)}, s32[1,4,256]{2,1,0:T(4,128)}, u32[]{:S(2)}) copy-start(s32[1,4,256]{2,1,0:T(4,128)} %reshape.596) | copy-start | bytes 12292
  89.4 5145.7 %copy-start.51 = (s32[256]{0:T(256)S(1)}, s32[256]{0:T(256)}, u32[]{:S(2)}) copy-start(s32[256]{0:T(256)} %copy-done.50) | copy-start | bytes 3076
  5391.0 150.4 %reduce-scatter.10.cloned.1.call-start = ((), (), s32[]{:S(2)}) async-start(), calls=%async_computation.13 | async-start | bytes 3538944 | tf_op jit(solution)/shard_map/reduce_scatter | solution.py:241
  5431.2 176.9 %reduce-scatter.16.cloned.1.call-start = ((), (), s32[]{:S(2)}) async-start(), calls=%async_computation.16 | async-start | bytes 1327104 | tf_op jit(solution)/shard_map/reduce_scatter | solution.py:274
  5434.2 107.2 %copy-start.37 = (f32[768]{0:T(1024)S(1)}, f32[768]{0:T(1024)}, u32[]{:S(2)}) copy-start(f32[768]{0:T(1024)} %copy-done.36) | copy-start | bytes 9220
  5434.2 107.2 %copy-start.54 = (f32[256]{0:T(256)S(1)}, f32[256]{0:T(256)}, u32[]{:S(2)}) copy-start(f32[256]{0:T(256)} %copy-done.53) | copy-start | bytes 3076
  5434.2 255.9 %reduce-scatter.14.cloned.1.call-start = ((), (), s32[]{:S(2)}) async-start(), calls=%async_computation.15 | async-start | bytes 3981312 | tf_op jit(solution)/shard_map/reduce_scatter | solution.py:271
  5443.5 102.3 %copy-start.9 = (bf16[1,4,128,3072]{3,2,1,0:T(8,128)(2,1)S(1)}, bf16[1,4,128,3072]{3,2,1,0:T(8,128)(2,1)}, u32[]{:S(2)}) copy-start(bf16[1,4,128,3072]{3,2,1,0:T(8,128)(2,1)} %fusion.12) | copy-start | bytes 9437188
  5545.8 461.1 %reduce-scatter.18.cloned.1.call-start = ((), (), s32[]{:S(2)}) async-start(), calls=%async_computation.17 | async-start | bytes 21233664 | tf_op jit(solution)/shard_map/reduce_scatter | solution.py:182
  5556.6 766.5 %reduce-scatter.20.cloned.1.call-start = ((), (), s32[]{:S(2)}) async-start(), calls=%async_computation.18 | async-start | bytes 21233664 | tf_op jit(solution)/shard_map/reduce_scatter | solution.py:185
  5570.1 753.1 %copy-start.11 = (s32[256,2048]{1,0:T(8,128)S(1)}, s32[256,2048]{1,0:T(8,128)}, u32[]{:S(2)}) copy-start(s32[256,2048]{1,0:T(8,128)} %copy-done.10) | copy-start | bytes 6291460
  5570.1 819.9 %reduce-scatter.22.cloned.1.call-start = ((), (), s32[]{:S(2)}) async-start(), calls=%async_computation.19 | async-start | bytes 221184
  5571.9 921.1 %all-reduce.10.cloned.1.call-start = ((), (), s32[]{:S(2)}) async-start(), calls=%async_computation.20 | async-start | bytes 10616832 | tf_op jit(solution)/shard_map/psum | solution.py:280
  (51 other events, 923.2 us)
Sparse Core Ops, SparseCore 0:
  10.2 68.0 all-gather.7
  82.8 58.9 all-gather.9
  144.5 59.0 all-gather.11
  205.6 39.6 all-gather.13
  246.7 361.2 all-gather.15
  609.4 362.4 all-gather.17
  5391.1 72.3 reduce-scatter.11
  5467.1 74.2 reduce-scatter.9
  5544.8 63.3 reduce-scatter.15
  5612.2 77.8 reduce-scatter.13
  5694.0 312.8 reduce-scatter.17
  6010.6 312.4 reduce-scatter.19
  6327.0 60.2 reduce-scatter.21
  6389.7 103.3 all-reduce.9
where the time goes:
time: 6520 us; the launch traced here: 6510 us
  local copies, waits for them, and re-layouts  5150 us (79%)
  waiting for transfers between devices  960 us (15%)
  matrix products  224 us (3%)
  blocking collectives  110 us (2%)
    gather x2, local copies, waits for them, and re-layouts, bucket_onehot(): pair_buckets = jnp.take(buckets, offsets, axis=0)  5120 us
    reduce_scatter x1, waiting for transfers between devices, body(): lax.psum_scatter(grad_w_up.astype(jnp.bfloat16), 'sp', scatter_dimension=...  317 us
    reduce_scatter x1, waiting for transfers between devices, body(): lax.psum_scatter(grad_w_down.astype(jnp.bfloat16), 'sp', scatter_dimensio...  316 us
  transfers between devices with their start and end apart: 14, of which 8 were waited for; matrix products, arithmetic and copies ran while one was open for 82% of the time, Pallas kernels for 0%

commit v1 on v0

v1 whole, which is shorter than its diff:
```python
import jax
import jax.numpy as jnp
from jax import lax
from jax.sharding import PartitionSpec as P

HIGHEST_PRECISION = lax.Precision.HIGHEST
epsilon = 1e-06


def rms_scale(values):
    return lax.rsqrt(jnp.mean(values * values, axis=-1, keepdims=True) + epsilon)


def norm_back(values, scale, gain, grad_out):
    weighted = gain * grad_out
    grad_in = scale * weighted - values * scale**3 * jnp.mean(
        weighted * values, axis=-1, keepdims=True
    )
    grad_gain = jnp.sum(grad_out * values * scale, axis=(0, 1))
    return (grad_in, grad_gain)


def toeplitz(window, rows, columns):
    inner = 16
    reach = columns + rows - inner
    near = jnp.stack([window[inner - 1 - b : inner - 1 - b + reach] for b in range(inner)])
    far = [
        near[:, rows - inner - inner * a : rows - inner - inner * a + columns]
        for a in range(rows // inner)
    ]
    return jnp.concatenate(far, axis=0)


def bucket_onehot(buckets, count, query_start, query_count, key_count):
    window = lax.dynamic_slice(
        buckets, (key_count - query_start - query_count,), (key_count + query_count - 1,)
    )
    pair_buckets = toeplitz(window, query_count, key_count)
    return (pair_buckets[:, :, None] == jnp.arange(count, dtype=jnp.int32)[None, None, :]).astype(
        jnp.bfloat16
    )


def columns_of(values):
    return jnp.pad(values, ((0, 0), (0, -values.shape[1] % 128)))


def split_heads(values, heads):
    return values.reshape(values.shape[0], values.shape[1], heads, values.shape[2] // heads)


def body(
    tokens,
    cotangent,
    routes,
    buckets,
    gain_attn,
    w_qkv,
    w_out,
    bias_table,
    gain_ffn,
    router,
    expert_in,
    expert_out,
):
    heads = bias_table.shape[1]
    bucket_count = bias_table.shape[0]
    seq_count, piece, width = tokens.shape
    experts = router.shape[1]
    sequences = lax.axis_size("dp")
    team = min(sequences, experts)
    share = experts // team
    first = lax.rem(lax.axis_index("dp"), team) * share
    teams = None
    if team < sequences:
        teams = [list(range(t, t + team)) for t in range(0, sequences, team)]
    packed = lax.all_gather(
        jnp.concatenate(
            (w_qkv, w_out, columns_of(jnp.concatenate((gain_attn[:, None], gain_ffn[:, None], router), 1))),
            axis=1,
        ),
        "sp",
        axis=0,
        tiled=True,
    )
    attn_set = (packed[:, 4 * width], packed[:, : 3 * width], packed[:, 3 * width : 4 * width])
    ffn_set = (
        packed[:, 4 * width + 1],
        packed[:, 4 * width + 2 : 4 * width + 2 + experts],
        lax.all_gather(
            lax.dynamic_slice_in_dim(expert_in, first, share, 0), "sp", axis=1, tiled=True
        ),
        lax.all_gather(
            lax.dynamic_slice_in_dim(expert_out, first, share, 0), "sp", axis=1, tiled=True
        ),
    )
    inputs = tokens.astype(jnp.float32)
    scale_one = rms_scale(inputs)
    normed_one = (inputs * scale_one * attn_set[0].astype(jnp.float32)).astype(jnp.bfloat16)
    projected = jnp.einsum(
        "spd,de->spe", normed_one, attn_set[1], preferred_element_type=jnp.float32
    ).astype(jnp.bfloat16)
    queries = projected[:, :, :width]
    keys_values = lax.all_gather(projected[:, :, width:], "sp", axis=1, tiled=True)
    keys_all, values_all = keys_values[:, :, :width], keys_values[:, :, width:]
    length = keys_all.shape[1]
    start = lax.axis_index("sp") * piece
    near_onehot = bucket_onehot(buckets, bucket_count, start, piece, length)
    bias_rows = jnp.einsum(
        "ijc,ch->hij", near_onehot, bias_table, preferred_element_type=jnp.float32
    )
    query_heads = split_heads(queries, heads)
    scores = (
        jnp.einsum(
            "sihd,sjhd->shij",
            query_heads,
            split_heads(keys_all, heads),
            preferred_element_type=jnp.float32,
        )
        + bias_rows[None]
    )
    top_score = jnp.max(scores, axis=-1, keepdims=True)
    log_total = top_score + jnp.log(jnp.sum(jnp.exp(scores - top_score), axis=-1, keepdims=True))
    probs_low = jnp.exp(scores - log_total).astype(jnp.bfloat16)
    attended = jnp.einsum(
        "shij,sjhd->sihd",
        probs_low,
        split_heads(values_all, heads),
        preferred_element_type=jnp.float32,
    )
    attended = attended.reshape(seq_count, piece, width).astype(jnp.bfloat16)
    middle = inputs + jnp.einsum(
        "spd,de->spe", attended, attn_set[2], preferred_element_type=jnp.float32
    )
    gain_two = ffn_set[0].astype(jnp.float32)
    scale_two = rms_scale(middle)
    normed_two = (middle * scale_two * gain_two).astype(jnp.bfloat16)
    logits = jnp.einsum("spd,de->spe", normed_two, ffn_set[1], preferred_element_type=jnp.float32)
    gates_all = jax.nn.softmax(logits, axis=-1)
    chosen_int = (routes == jnp.arange(experts, dtype=jnp.int32)[None, None, :]).astype(jnp.int32)
    chosen = chosen_int.astype(jnp.float32)
    gate = jnp.sum(gates_all * chosen, axis=-1, keepdims=True)
    capacity = 2 * piece // experts
    place = jnp.sum((jnp.cumsum(chosen_int, axis=1) - 1) * chosen_int, axis=-1)
    slots = (place[:, :, None] == jnp.arange(capacity, dtype=jnp.int32)[None, None, :]).astype(
        jnp.float32
    )
    dispatch_low = (chosen[:, :, :, None] * slots[:, :, None, :]).astype(jnp.bfloat16)
    grad_out = cotangent.astype(jnp.float32)
    grad_returned = (gate * grad_out).astype(jnp.bfloat16)
    sent = jnp.einsum(
        "stec,std->escd",
        dispatch_low,
        jnp.concatenate((normed_two, grad_returned), axis=-1),
        preferred_element_type=jnp.float32,
    ).astype(jnp.bfloat16)
    held = lax.all_to_all(
        sent.reshape(experts, seq_count * capacity, 2 * width),
        "dp",
        0,
        1,
        axis_index_groups=teams,
        tiled=True,
    )
    buffers, grad_outs = held[:, :, :width], held[:, :, width:]
    hidden_in = jnp.einsum("ecd,edf->ecf", buffers, ffn_set[2], preferred_element_type=jnp.float32)
    activated = jax.nn.gelu(hidden_in).astype(jnp.bfloat16)
    expert_outs = jnp.einsum(
        "ecf,efd->ecd", activated, ffn_set[3], preferred_element_type=jnp.float32
    )
    grad_act = jnp.einsum(
        "ecd,efd->ecf", grad_outs, ffn_set[3], preferred_element_type=jnp.float32
    )
    grad_hidden = jax.vjp(jax.nn.gelu, hidden_in)[1](grad_act)[0].astype(jnp.bfloat16)
    grad_buffers = jnp.einsum(
        "ecf,edf->ecd", grad_hidden, ffn_set[2], preferred_element_type=jnp.float32
    )
    back = lax.all_to_all(
        jnp.concatenate((expert_outs, grad_buffers), axis=-1).astype(jnp.bfloat16),
        "dp",
        1,
        0,
        axis_index_groups=teams,
        tiled=True,
    )
    grad_w_down = jnp.einsum(
        "ecf,ecd->efd", activated, grad_outs, preferred_element_type=jnp.float32
    )
    grad_w_up = jnp.einsum(
        "ecd,ecf->edf", buffers, grad_hidden, preferred_element_type=jnp.float32
    )
    taken = jnp.einsum(
        "stec,escd->std",
        dispatch_low,
        back.reshape(experts, seq_count, capacity, 2 * width),
        preferred_element_type=jnp.float32,
    )
    returned, grad_normed_two = taken[:, :, :width], taken[:, :, width:]
    mixed = (middle + gate * returned).astype(jnp.bfloat16)
    grad_gate = jnp.sum(grad_out * returned, axis=-1, keepdims=True)
    grad_logits = grad_gate * gate * (chosen - gates_all)
    grad_router = jnp.einsum(
        "spd,spe->de", normed_two.astype(jnp.float32), grad_logits, precision=HIGHEST_PRECISION
    )
    grad_normed_two = grad_normed_two + jnp.einsum(
        "spe,de->spd", grad_logits, ffn_set[1].astype(jnp.float32), precision=HIGHEST_PRECISION
    )
    grad_middle, grad_gain_two = norm_back(
        middle, scale_two, ffn_set[0].astype(jnp.float32), grad_normed_two
    )
    grad_middle = grad_out + grad_middle
    grad_branch = grad_middle.astype(jnp.bfloat16)
    grad_w_out = jnp.einsum(
        "spd,spe->de", attended, grad_branch, preferred_element_type=jnp.float32
    )
    up_share = lax.psum_scatter(
        grad_w_up.astype(jnp.bfloat16), "sp", scatter_dimension=1, tiled=True
    )
    down_share = lax.psum_scatter(
        grad_w_down.astype(jnp.bfloat16), "sp", scatter_dimension=1, tiled=True
    )
    early = lax.psum_scatter(
        jnp.concatenate(
            (
                grad_w_out.astype(jnp.bfloat16),
                columns_of(
                    jnp.concatenate((grad_gain_two[:, None], grad_router), 1).astype(jnp.bfloat16)
                ),
            ),
            axis=1,
        ),
        "sp",
        scatter_dimension=0,
        tiled=True,
    )
    grad_attended = jnp.einsum(
        "spe,de->spd", grad_branch, attn_set[2], preferred_element_type=jnp.float32
    ).astype(jnp.bfloat16)
    grad_heads = split_heads(grad_attended, heads)
    key_heads = split_heads(keys_all, heads)
    value_heads = split_heads(values_all, heads)
    scores_back = (
        jnp.einsum("sihd,sjhd->shij", query_heads, key_heads, preferred_element_type=jnp.float32)
        + bias_rows[None]
    )
    probs_back = jnp.exp(scores_back - log_total)
    grad_probs = jnp.einsum(
        "sihd,sjhd->shij", grad_heads, value_heads, preferred_element_type=jnp.float32
    )
    row_dot = jnp.sum(probs_back * grad_probs, axis=-1, keepdims=True)
    grad_scores = (probs_back * (grad_probs - row_dot)).astype(jnp.bfloat16)
    grad_queries = jnp.einsum(
        "shij,sjhd->sihd", grad_scores, key_heads, preferred_element_type=jnp.float32
    )
    grad_queries = grad_queries.reshape(seq_count, piece, width).astype(jnp.bfloat16)
    grad_table = jnp.einsum(
        "shij,ijc->ch", grad_scores, near_onehot, preferred_element_type=jnp.float32
    )
    grad_keys_part = jnp.einsum(
        "shij,sihd->sjhd", grad_scores, query_heads, preferred_element_type=jnp.float32
    )
    grad_values_part = jnp.einsum(
        "shij,sihd->sjhd",
        probs_back.astype(jnp.bfloat16),
        grad_heads,
        preferred_element_type=jnp.float32,
    )
    grad_keys_values = lax.psum_scatter(
        jnp.concatenate(
            (
                grad_keys_part.reshape(seq_count, length, width),
                grad_values_part.reshape(seq_count, length, width),
            ),
            axis=-1,
        ).astype(jnp.bfloat16),
        "sp",
        scatter_dimension=1,
        tiled=True,
    )
    grad_projected = jnp.concatenate((grad_queries, grad_keys_values), axis=-1)
    grad_w_qkv = jnp.einsum(
        "spd,spe->de", normed_one, grad_projected, preferred_element_type=jnp.float32
    )
    grad_normed_one = jnp.einsum(
        "spe,de->spd", grad_projected, attn_set[1], preferred_element_type=jnp.float32
    )
    grad_inputs, grad_gain_one = norm_back(
        inputs, scale_one, attn_set[0].astype(jnp.float32), grad_normed_one
    )
    grad_inputs = grad_middle + grad_inputs
    late = lax.psum_scatter(
        jnp.concatenate(
            (grad_w_qkv.astype(jnp.bfloat16), columns_of(grad_gain_one[:, None].astype(jnp.bfloat16))),
            axis=1,
        ),
        "sp",
        scatter_dimension=0,
        tiled=True,
    )
    grad_up, grad_down = (
        jnp.sum(
            lax.all_gather(each, "dp", axis=0, tiled=True)
            .reshape(sequences // team, experts, *each.shape[1:])
            .astype(jnp.float32),
            axis=0,
        )
        for each in (up_share, down_share)
    )
    early = lax.psum(early, "dp").astype(jnp.float32)
    late = lax.psum(late, "dp").astype(jnp.float32)
    table_total = lax.psum(grad_table, ("dp", "sp"))
    return (
        mixed,
        grad_inputs,
        late[:, 3 * width],
        late[:, : 3 * width],
        early[:, :width],
        table_total,
        early[:, width],
        early[:, width + 1 : width + 1 + experts],
        grad_up,
        grad_down,
    )


def solution(mesh):
    return jax.shard_map(
        body,
        mesh=mesh,
        in_specs=(
            P("dp", "sp", None),
            P("dp", "sp", None),
            P("dp", "sp", None),
            P(),
            P("sp"),
            P("sp", None),
            P("sp", None),
            P(),
            P("sp"),
            P("sp", None),
            P(None, "sp", None),
            P(None, "sp", None),
        ),
        out_specs=(
            P("dp", "sp", None),
            P("dp", "sp", None),
            P("sp"),
            P("sp", None),
            P("sp", None),
            P(),
            P("sp"),
            P("sp", None),
            P(None, "sp", None),
            P(None, "sp", None),
        ),
        check_vma=False,
    )
```

time: 6520 us -> 945 us (0.14)
  local copies, waits for them, and re-layouts: 5150 us -> 60.9 us
  waiting for transfers between devices: 960 us -> 524 us
    gather x2 -> x0, local copies, waits for them, and re-layouts: 5120 us -> none  [bucket_onehot(): pair_buckets = jnp.take(buckets, offsets, axis=0)]
    reduce_scatter x1, waiting for transfers between devices: 316 us -> 0.02 us  [body(): lax.psum_scatter(grad_w_down.astype(jnp.bfloat16), 'sp', scatter_dimensio...]
    reduce_scatter x1, waiting for transfers between devices: 317 us -> 51.9 us  [body(): lax.psum_scatter(grad_w_up.astype(jnp.bfloat16), 'sp', scatter_dimension=...]
    all_gather x6, waiting for transfers between devices: 41.2 us -> 244 us  [the longest x1 83.8 us: body(): lax.all_gather(jnp.concatenate((w_qkv, w_out, columns_of(jnp.concatenate(...]
    reduce_scatter x4 -> x2, waiting for transfers between devices: 215 us -> 193 us  [the longest x1 112 us: body(): lax.psum_scatter(jnp.concatenate((grad_keys_part.reshape(seq_count, lengt...]
  transfers between devices with their start and end apart: 14 -> 12, of which waited for: 8 -> 9; matrix products, arithmetic and copies ran while one was open for 82% -> 30% of each run, Pallas kernels for 0% -> 0%
where the time goes in v1:
time: 945 us; the launch traced here: 934 us
  waiting for transfers between devices  524 us (55%)
  matrix products  177 us (19%)
  blocking collectives  85.9 us (9%)
  other arithmetic  70.5 us (7%)
  local copies, waits for them, and re-layouts  60.9 us (6%)
  between operations  15.4 us (2%)
    reduce_scatter x1, waiting for transfers between devices, body(): lax.psum_scatter(jnp.concatenate((grad_keys_part.reshape(seq_count, lengt...  112 us
    all_gather x1, waiting for transfers between devices, body(): lax.all_gather(jnp.concatenate((w_qkv, w_out, columns_of(jnp.concatenate(...  83.8 us
    reduce_scatter x1, waiting for transfers between devices, body(): lax.psum_scatter(jnp.concatenate((grad_w_qkv.astype(jnp.bfloat16), column...  81.3 us
    all_gather x1, waiting for transfers between devices, body(): lax.all_gather(projected[:, :, width:], 'sp', axis=1, tiled=True)  73 us
    reduce_scatter x1, waiting for transfers between devices, body(): lax.psum_scatter(grad_w_up.astype(jnp.bfloat16), 'sp', scatter_dimension=...  51.9 us
    all_gather x1, waiting for transfers between devices, body(): lax.all_gather(lax.dynamic_slice_in_dim(expert_out, first, share, 0), 'sp...  51.4 us
    psum x1, blocking collectives, body(): table_total = lax.psum(grad_table, ('dp', 'sp'))  39.7 us
    all_gather x2, waiting for transfers between devices, body(): lax.all_gather(each, 'dp', axis=0, tiled=True)  35.5 us
  transfers between devices with their start and end apart: 12, of which 9 were waited for; matrix products, arithmetic and copies ran while one was open for 30% of the time, Pallas kernels for 0%

profile of v1, /device:TPU:0, one launch (start us, length us, event | category | flops | bytes accessed | tf_op | source)
XLA Modules:
  0.0 934.0 jit_solution(9701722298772108671)
XLA Ops:
  12.0 83.8 %all-gather.7.cloned.1.call-done = bf16[768,3200]{1,0:T(8,128)(2,1)} async-done(((bf16[96,3200]{1,0:T(8,128)(2,1)}), bf16[768,3200]{1,0:T(8,128)(2,1)}) %all-gather.7.cloned.1.call-update) | async-done | bytes 4915216 | tf_op jit(solution)/shard_map/all_gather | solution.py:77
  111.5 15.1 %fusion.1 = f32[256,2048,12]{1,2,0:T(8,128)} fusion(s32[256,2048]{1,0:T(8,128)S(1)} %slice_dynamic-update-slice_fusion, bf16[32,12]{0,1:T(8,128)(2,1)S(1)} %copy-done.51), kind=kOutput, calls=%fused_computation.2 | convolution fusion | flops 419430400 | bytes 27263744 | tf_op jit(solution)/shard_map/ijc,ch->hij/dot_general | solution.py:109
  127.8 73.0 %all-gather.9.cloned.1.call-done = bf16[1,2048,1536]{2,1,0:T(8,128)(2,1)} async-done(((bf16[1,256,1536]{2,1,0:T(8,128)(2,1)}), bf16[1,2048,1536]{2,1,0:T(8,128)(2,1)}) %all-gather.9.cloned.1.call-update) | async-done | bytes 6291472 | tf_op jit(solution)/shard_map/all_gather | solution.py:104
  216.4 28.7 %fusion.106 = (f32[12,256]{1,0:T(8,128)S(1)}, f32[12,256,2048]{2,1,0:T(8,128)}) fusion(f32[256,2048,12]{1,2,0:T(8,128)} %fusion.1, bf16[256,12,64]{0,2,1:T(8,128)(2,1)S(1)} %bitcast.164, bf16[2048,12,64]{0,2,1:T(8,128)(2,1)} %bitcast.157), kind=kOutput, calls=%fused_computation.174 | convolution fusion | flops 817886208 | bytes 53882880 | tf_op jit(solution)/shard_map/sihd,sjhd->shij/dot_general | solution.py:114
  245.1 11.0 %exponential_reduce_fusion = f32[12,256]{1,0:T(8,128)S(1)} fusion(f32[12,256,2048]{2,1,0:T(8,128)} %get-tuple-element.83, f32[12,256]{1,0:T(8,128)S(1)} %get-tuple-element.82), kind=kLoop, calls=%fused_computation.9 | loop fusion | flops 12579840 | bytes 25190400 | tf_op jit(solution)/shard_map/reduce_sum | solution.py:123
  256.1 10.4 %fusion.48 = bf16[12,64,256]{2,1,0:T(8,128)(2,1)S(1)} fusion(bf16[2048,12,64]{0,2,1:T(8,128)(2,1)S(1)} %bitcast.156, f32[12,256,2048]{2,1,0:T(8,128)} %get-tuple-element.83, f32[12,256]{1,0:T(8,128)S(1)} %log_add_fusion), kind=kOutput, calls=%fused_computation.67 | convolution fusion | flops 818085888 | bytes 28717056 | tf_op jit(solution)/shard_map/shij,sjhd->sihd/dot_general | solution.py:125
  273.8 22.6 %all_to_all.21 = bf16[4,128,1536]{1,2,0:T(8,128)(2,1)S(1)} all-to-all(bf16[4,128,1536]{1,2,0:T(8,128)(2,1)S(1)} %fusion.34), channel_id=1, replica_groups=mesh['dp'=4,'sp'=8] {'dp'}, dimensions={0} | all-to-all | bytes 3145728 | tf_op jit(solution)/shard_map/all_to_all | solution.py:157
  310.5 51.4 %all-gather.13.cloned.1.call-done = bf16[1,3072,768]{2,1,0:T(8,128)(2,1)} async-done(((bf16[1,384,768]{2,1,0:T(8,128)(2,1)}), bf16[1,3072,768]{2,1,0:T(8,128)(2,1)}) %all-gather.13.cloned.1.call-update) | async-done | bytes 4718608 | tf_op jit(solution)/shard_map/all_gather | solution.py:93
  361.8 8.7 fusion.13
  376.8 8.1 fusion.41
  394.7 11.7 %reduce.24 = bf16[512,1536]{1,0:T(8,128)(2,1)S(1)} reduce(bf16[512,1,1536]{2,1,0:T(2,128)(2,1)} %bitcast.161, bf16[]{:T(256)} %broadcast.259), dimensions={1}, to_apply=%bitcast.154.reduce_sub_computation | reduce | bytes 3145730
  408.8 23.6 %all_to_all.22 = bf16[4,2,98304]{2,1,0:T(2,128)(2,1)S(1)} all-to-all(bf16[4,2,98304]{2,1,0:T(2,128)(2,1)} %reshape.658), channel_id=1, replica_groups=mesh['dp'=4,'sp'=8] {'dp'}, dimensions={0} | all-to-all | bytes 3145728 | tf_op jit(solution)/shard_map/all_to_all | solution.py:178
  443.8 16.8 %multiply_reduce_fusion = (f32[12,256]{1,0:T(8,128)S(1)}, f32[12,256,2048]{2,1,0:T(8,128)}) fusion(f32[12,256,2048]{2,1,0:T(8,128)} %get-tuple-element.83, f32[12,256]{1,0:T(8,128)S(1)} %log_add_fusion, bf16[256,12,64]{0,2,1:T(8,128)(2,1)S(1)} %bitcast.166, bf16[2048,12,64]{0,2,1:T(8,128)(2,1)} %bitcast.155), kind=kOutput, calls=%fused_computation.7 | convolution fusion | flops 824177664 | bytes 53895168 | tf_op jit(solution)/shard_map/sihd,sjhd->shij/dot_general | solution.py:247
  460.6 17.0 %multiply_convert_fusion = bf16[12,256,2048]{2,1,0:T(8,128)(2,1)S(1)} fusion(f32[12,256,2048]{2,1,0:T(8,128)} %get-tuple-element.90, f32[12,256,2048]{2,1,0:T(8,128)} %get-tuple-element.83, f32[12,256]{1,0:T(8,128)S(1)} %get-tuple-element.89, f32[12,256]{1,0:T(8,128)S(1)} %log_add_fusion), kind=kLoop, calls=%fused_computation.6 | loop fusion | flops 25165824 | bytes 62939136 | tf_op jit(solution)/shard_map/convert_element_type | solution.py:251
  484.5 12.4 %convolution_convert_fusion.4 = bf16[12,64,2048]{2,1,0:T(8,128)(2,1)} fusion(bf16[256,12,64]{0,2,1:T(8,128)(2,1)S(1)} %bitcast.167, f32[12,256,2048]{2,1,0:T(8,128)} %get-tuple-element.83, f32[12,256]{1,0:T(8,128)S(1)} %log_add_fusion), kind=kOutput, calls=%fused_computation.41 | convolution fusion | flops 819462144 | bytes 28717056 | tf_op jit(solution)/shard_map/shij,sihd->sjhd/dot_general | solution.py:262
  506.7 51.9 %reduce-scatter.12.cloned.1.call-done = bf16[1,96,3072]{2,1,0:T(8,128)(2,1)} async-done(((bf16[1,768,3072]{2,1,0:T(8,128)(2,1)}), bf16[1,96,3072]{2,1,0:T(8,128)(2,1)}) %reduce-scatter.12.cloned.1.call-update) | async-done | bytes 589840 | tf_op jit(solution)/shard_map/reduce_scatter | solution.py:216
  558.7 9.5 %convolution_convert_fusion.9 = bf16[12,64,256]{2,1,0:T(8,128)(2,1)S(1)} fusion(bf16[2048,12,64]{0,2,1:T(8,128)(2,1)} %bitcast.158, bf16[12,256,2048]{2,1,0:T(8,128)(2,1)} %copy-done.2), kind=kOutput, calls=%fused_computation.68 | convolution fusion | flops 805502976 | bytes 16121856 | tf_op jit(solution)/shard_map/shij,sjhd->sihd/dot_general | solution.py:252
  568.2 112.0 %reduce-scatter.8.cloned.1.call-done = bf16[1,256,1536]{1,2,0:T(8,128)(2,1)} async-done(((bf16[1,2048,1536]{1,2,0:T(8,128)(2,1)}), bf16[1,256,1536]{1,2,0:T(8,128)(2,1)}) %reduce-scatter.8.cloned.1.call-update) | async-done | bytes 786448 | tf_op jit(solution)/shard_map/reduce_scatter | solution.py:268
  689.7 26.9 %fusion.52 = f32[32,12]{0,1:T(8,128)S(1)} fusion(bf16[12,256,2048]{2,1,0:T(8,128)(2,1)} %copy-done.2, s32[256,2048]{1,0:T(8,128)S(1)} %copy-done.5), kind=kOutput, calls=%fused_computation.76 | convolution fusion | flops 419430400 | bytes 14681600 | tf_op jit(solution)/shard_map/shij,ijc->ch/dot_general | solution.py:256
  716.6 39.7 %psum.23 = f32[32,12]{0,1:T(8,128)} all-reduce(f32[32,12]{0,1:T(8,128)S(1)} %fusion.52), channel_id=1, replica_groups=mesh['dp'=4,'sp'=8] {'dp','sp'}, use_global_device_ids=true, to_apply=%region_21.22 | all-reduce | flops 384 | bytes 3072 | tf_op jit(solution)/shard_map/psum | solution.py:311
  758.1 14.3 %all-gather.17.cloned.1.call-done = bf16[4,384,768]{2,1,0:T(8,128)(2,1)} async-done(((bf16[1,384,768]{2,1,0:T(8,128)(2,1)}), bf16[4,384,768]{2,1,0:T(8,128)(2,1)}) %all-gather.17.cloned.1.call-update) | async-done | bytes 2359312 | tf_op jit(solution)/shard_map/all_gather | solution.py:302
  776.6 21.3 %all-gather.15.cloned.1.call-done = bf16[4,96,3072]{2,1,0:T(8,128)(2,1)} async-done(((bf16[1,96,3072]{2,1,0:T(8,128)(2,1)}), bf16[4,96,3072]{2,1,0:T(8,128)(2,1)}) %all-gather.15.cloned.1.call-update) | async-done | bytes 2359312 | tf_op jit(solution)/shard_map/all_gather | solution.py:302
  802.3 81.3 %reduce-scatter.10.cloned.1.call-done = bf16[96,2432]{1,0:T(8,128)(2,1)} async-done(((bf16[768,2432]{1,0:T(8,128)(2,1)}), bf16[96,2432]{1,0:T(8,128)(2,1)}) %reduce-scatter.10.cloned.1.call-update) | async-done | bytes 466960 | tf_op jit(solution)/shard_map/reduce_scatter | solution.py:291
  886.1 34.1 %all-reduce.6.cloned.1.call-done = (bf16[96,2432]{1,0:T(8,128)(2,1)}, bf16[96,896]{0,1:T(8,128)(2,1)}) async-done(((bf16[96,2432]{1,0:T(8,128)(2,1)}, bf16[96,896]{0,1:T(8,128)(2,1)}), (bf16[96,2432]{1,0:T(8,128)(2,1)}, bf16[96,896]{0,1:T(8,128)(2,1)})) %all-reduce.6.cloned.1.call-update) | async-done | bytes 638992 | tf_op jit(solution)/shard_map/psum | solution.py:310
  (253 shorter events, 133.2 us)
Async XLA Ops:
  7.2 96.4 %copy-start = (bf16[4,96,3072]{2,1,0:T(8,128)(2,1)S(1)}, bf16[4,96,3072]{2,1,0:T(8,128)(2,1)}, u32[]{:S(2)}) copy-start(bf16[4,96,3072]{2,1,0:T(8,128)(2,1)} %param.22) | copy-start | bytes 7077892
  7.2 88.6 %all-gather.7.cloned.1.call-start = ((), (), s32[]{:S(2)}) async-start(), calls=%async_computation.7 | async-start | bytes 5529600 | tf_op jit(solution)/shard_map/all_gather | solution.py:77
  10.2 190.7 %all-gather.9.cloned.1.call-start = ((), (), s32[]{:S(2)}) async-start(), calls=%async_computation.8 | async-start | bytes 7077888 | tf_op jit(solution)/shard_map/all_gather | solution.py:104
  12.0 85.7 %copy-start.46 = (f32[256]{0:T(256)}, f32[256]{0:T(256)S(1)}, u32[]{:S(2)}) copy-start(f32[256]{0:T(256)S(1)} %get-tuple-element.79) | copy-start | bytes 3076
  103.5 194.5 %all-gather.11.cloned.1.call-start = ((), (), s32[]{:S(2)}) async-start(), calls=%async_computation.9 | async-start | bytes 5308416 | tf_op jit(solution)/shard_map/all_gather | solution.py:90
  104.5 257.4 %all-gather.13.cloned.1.call-start = ((), (), s32[]{:S(2)}) async-start(), calls=%async_computation.10 | async-start | bytes 5308416 | tf_op jit(solution)/shard_map/all_gather | solution.py:93
  106.5 399.6 %reduce-scatter.14.cloned.1.call-start = ((), (), s32[]{:S(2)}) async-start(), calls=%async_computation.15 | async-start | bytes 5308416 | tf_op jit(solution)/shard_map/reduce_scatter | solution.py:219
  107.9 164.7 %copy-start.40 = (f32[256,4]{0,1:T(4,128)}, f32[256,4]{0,1:T(4,128)S(1)}, u32[]{:S(2)}) copy-start(f32[256,4]{0,1:T(4,128)S(1)} %convert_convert_fusion) | copy-start | bytes 12292
  110.2 16.5 %copy-start.4 = (s32[256,2048]{1,0:T(8,128)}, s32[256,2048]{1,0:T(8,128)S(1)}, u32[]{:S(2)}) copy-start(s32[256,2048]{1,0:T(8,128)S(1)} %slice_dynamic-update-slice_fusion) | copy-start | bytes 6291460
  245.1 11.1 %copy-start.3 = (bf16[1,2048,768]{1,2,0:T(8,128)(2,1)S(1)}, bf16[1,2048,768]{1,2,0:T(8,128)(2,1)}, u32[]{:S(2)}) copy-start(bf16[1,2048,768]{1,2,0:T(8,128)(2,1)} %copy.65) | copy-start | bytes 9437188
  256.1 10.5 %copy-start.8 = (bf16[1,256,768]{2,1,0:T(8,128)(2,1)S(1)}, bf16[1,256,768]{2,1,0:T(8,128)(2,1)}, u32[]{:S(2)}) copy-start(bf16[1,256,768]{2,1,0:T(8,128)(2,1)} %param.12) | copy-start | bytes 1179652
  256.1 13.6 %copy-start.24 = (f32[768]{0:T(1024)S(1)}, f32[768]{0:T(1024)}, u32[]{:S(2)}) copy-start(f32[768]{0:T(1024)} %get-tuple-element.50) | copy-start | bytes 9220
  310.4 248.2 %reduce-scatter.12.cloned.1.call-start = ((), (), s32[]{:S(2)}) async-start(), calls=%async_computation.13 | async-start | bytes 5308416 | tf_op jit(solution)/shard_map/reduce_scatter | solution.py:216
  376.6 303.6 %reduce-scatter.8.cloned.1.call-start = ((), (), s32[]{:S(2)}) async-start(), calls=%async_computation.11 | async-start | bytes 7077888 | tf_op jit(solution)/shard_map/reduce_scatter | solution.py:268
  502.4 254.0 %reduce-scatter.16.cloned.1.call-start = ((), (), s32[]{:S(2)}) async-start(), calls=%async_computation.17 | async-start | bytes 1548288
  505.9 266.5 %all-gather.17.cloned.1.call-start = ((), (), s32[]{:S(2)}) async-start(), calls=%async_computation.16 | async-start | bytes 2949120 | tf_op jit(solution)/shard_map/all_gather | solution.py:302
  506.7 291.2 %all-gather.15.cloned.1.call-start = ((), (), s32[]{:S(2)}) async-start(), calls=%async_computation.14 | async-start | bytes 2949120 | tf_op jit(solution)/shard_map/all_gather | solution.py:302
  558.6 121.6 %copy-start.9 = (bf16[1,256,768]{2,1,0:T(8,128)(2,1)S(1)}, bf16[1,256,768]{2,1,0:T(8,128)(2,1)}, u32[]{:S(2)}) copy-start(bf16[1,256,768]{2,1,0:T(8,128)(2,1)} %param.12) | copy-start | bytes 1179652
  558.6 121.6 %copy-start.31 = (f32[768]{0:T(1024)S(1)}, f32[768]{0:T(1024)}, u32[]{:S(2)}) copy-start(f32[768]{0:T(1024)} %copy-done.30) | copy-start | bytes 9220
  558.7 121.5 %copy-start.47 = (f32[256]{0:T(256)S(1)}, f32[256]{0:T(256)}, u32[]{:S(2)}) copy-start(f32[256]{0:T(256)} %copy-done.46) | copy-start | bytes 3076
  558.7 324.9 %reduce-scatter.10.cloned.1.call-start = ((), (), s32[]{:S(2)}) async-start(), calls=%async_computation.12 | async-start | bytes 4202496 | tf_op jit(solution)/shard_map/reduce_scatter | solution.py:291
  688.1 232.1 %all-reduce.6.cloned.1.call-start = ((), (), s32[]{:S(2)}) async-start(), calls=%async_computation.18 | async-start | bytes 1392640 | tf_op jit(solution)/shard_map/psum | solution.py:310
  776.6 107.0 %copy-start.49 = (f32[256]{0:T(256)S(1)}, f32[256]{0:T(256)}, u32[]{:S(2)}) copy-start(f32[256]{0:T(256)} %get-tuple-element.78) | copy-start | bytes 3076
  883.6 43.3 %copy-start.1 = (bf16[4,96,3072]{2,1,0:T(8,128)(2,1)S(1)}, bf16[4,96,3072]{2,1,0:T(8,128)(2,1)}, u32[]{:S(2)}) copy-start(bf16[4,96,3072]{2,1,0:T(8,128)(2,1)} %param.22) | copy-start | bytes 7077892
  (43 other events, 120.0 us)
Sparse Core Ops, SparseCore 0:
  10.8 84.9 all-gather.6
  103.6 97.1 all-gather.8
  203.7 78.0 all-gather.10
  283.8 78.0 all-gather.12
  365.9 93.3 reduce-scatter.13
  463.4 95.1 reduce-scatter.11
  562.2 117.9 reduce-scatter.7
  683.6 63.9 reduce-scatter.15
  749.1 23.2 all-gather.16
  773.8 24.0 all-gather.14
  801.6 81.9 reduce-scatter.9
  886.5 33.7 all-reduce.5
